TPU v7x, 32 devices: a whole 2x2x4 slice. The times are simulated.
32 devices in a mesh: blk: 8 (over z, x), win: 4 (over y, core).
Axes of the slice: x: 2, y: 2, z: 4, core: 2. Of those that a mesh axis runs over, the one named last changes fastest.
Arguments:
- traces: bfloat16 [2048, 4, 1024], P('blk', 'win')
- pairs: int32 [8, 2], P('blk'), may hold values from -1 to 15, as said below
Outputs:
- cross: float32 [8, 2, 48, 128, 128], P('blk', None, 'win')
Inputs may be any that keep to these rules, and one draw needn't show every extreme that they name: `pairs`: each live pair slot names two blocks held by its owning blk index or by the blk indices just below or just above it. Empty slots hold -1 in both entries.
All inputs are finite; a program needn't handle non-finite values.
Results may differ from a plain program's by a relative error of at most 0.0051.
Values may be sent and summed in bfloat16 or wider, within the bound.
A program may use at most 64 MiB of HBM per device.

v0:
```python
import math

import jax
import jax.numpy as jnp
from jax import lax
from jax.sharding import PartitionSpec as P

CH = 128
BINS = 48
FIRST_BIN = 8


def with_halo(cells, sides, width):
    for axis, dim in sides:
        count = lax.axis_size(axis)
        ends = count - 1
        head = lax.slice_in_dim(cells, 0, width, axis=dim)
        tail = lax.slice_in_dim(cells, cells.shape[dim] - width, cells.shape[dim], axis=dim)
        cells = jnp.concatenate(
            [
                lax.ppermute(tail, axis, [(i, (i + 1) % count) for i in range(ends)]),
                cells,
                lax.ppermute(head, axis, [((i + 1) % count, i) for i in range(ends)]),
            ],
            axis=dim,
        )
    return cells


def spectra_table(samples, bins):
    times = jnp.arange(samples, dtype=jnp.int32)[:, None]
    freqs = FIRST_BIN + jnp.arange(bins, dtype=jnp.int32)[None, :]
    phase = (times * freqs % samples).astype(jnp.float32) * (2.0 * math.pi / samples)
    return jnp.stack([jnp.cos(phase), -jnp.sin(phase)], 1).astype(jnp.bfloat16)


def cross_pair(first, second):
    left = jnp.concatenate([first[:, 0], first[:, 1]], 0)
    turned_left = jnp.concatenate([first[:, 1], first[:, 0]], 0)
    right = jnp.concatenate([second[:, 0], second[:, 1]], 0)
    turned_right = jnp.concatenate([second[:, 0], -second[:, 1]], 0)
    real_part = jnp.einsum("kfi,kfj->fij", left, right, preferred_element_type=jnp.float32)
    imag_part = jnp.einsum(
        "kfi,kfj->fij", turned_left, turned_right, preferred_element_type=jnp.float32
    )
    return jnp.stack([real_part, imag_part])


def correlate(wide, pairs, blocks_here):
    lowest = (lax.axis_index("blk") - 1) * blocks_here
    limit = 3 * blocks_here - 1

    def one_pair(pair):
        start_a = jnp.clip(pair[0] - lowest, 0, limit) * CH
        start_b = jnp.clip(pair[1] - lowest, 0, limit) * CH
        first = lax.dynamic_slice_in_dim(wide, start_a, CH, 3)
        second = lax.dynamic_slice_in_dim(wide, start_b, CH, 3)
        return cross_pair(first, second)

    return lax.map(one_pair, pairs)


def shards(traces, pairs):
    table = spectra_table(traces.shape[2], BINS)
    spec = jnp.einsum("rwt,tcf->wcfr", traces, table, preferred_element_type=jnp.float32)
    energy = jnp.mean(spec * spec, axis=(1, 2))
    whitened = (spec * lax.rsqrt(energy + 1e-06)[:, None, None, :]).astype(jnp.bfloat16)
    own_rows = whitened.shape[3]
    blocks_here = own_rows // CH
    windows_all = whitened.shape[0] * lax.axis_size("win")
    wide = with_halo(whitened, (("blk", 3),), own_rows)
    partial_value = correlate(wide, pairs, blocks_here)
    summed = lax.psum_scatter(partial_value, "win", scatter_dimension=2, tiled=True)
    live = (pairs[:, 0] >= 0).astype(jnp.float32)
    return summed * (1.0 / math.sqrt(windows_all)) * live[:, None, None, None, None]


def solution(mesh):
    placed = (P("blk", "win", None), P("blk", None))
    return jax.shard_map(
        shards,
        mesh=mesh,
        in_specs=placed,
        out_specs=P("blk", None, "win", None, None),
        check_vma=False,
    )
```

profile of v0, /device:TPU:0, one launch (start us, length us, event | category | flops | bytes accessed | tf_op | source)
XLA Modules:
  0.0 153.7 jit_solution(15617953487481813598)
XLA Ops:
  6.5 0.0 copy-start
  6.5 0.0 all-reduce.3.cloned.1.call-start
  6.5 0.9 cosine_convert_fusion
  7.4 0.2 copy-done
  7.6 0.3 multiply_reduce_fusion
  7.9 4.8 %collective-permute-start = (bf16[1,2,48,256]{3,2,1,0:T(8,128)(2,1)S(1)}, bf16[1,2,48,256]{3,2,1,0:T(8,128)(2,1)S(1)}, u32[]{:S(2)}, u32[]{:S(2)}) collective-permute-start(bf16[1,2,48,256]{3,2,1,0:T(8,128)(2,1)S(1)} %fusion.11), channel_id=1, source_target_pairs={{0,4},{4,8},{8,12},{12,16},{16,20},{20,24},{24,28},{1,5},{5,9},{9,... | collective-permute-start | bytes 147464 | tf_op jit(solution)/shard_map/ppermute | solution.py:21
  12.8 1.3 collective-permute-start.1
  14.1 1.3 fusion.18
  16.6 0.0 collective-permute-done
  16.6 2.1 %collective-permute-done.1 = bf16[1,2,48,256]{3,2,1,0:T(8,128)(2,1)S(1)} collective-permute-done((bf16[1,2,48,256]{3,2,1,0:T(8,128)(2,1)S(1)}, bf16[1,2,48,256]{3,2,1,0:T(8,128)(2,1)S(1)}, u32[]{:S(2)}, u32[]{:S(2)}) %collective-permute-start.1) | collective-permute-done | bytes 49184 | tf_op jit(solution)/shard_map/ppermute | solution.py:23
  18.8 0.6 convolution_bitcast_fusion.1
  19.5 0.6 convolution_bitcast_fusion
  20.1 3.1 %maximum_bitcast_fusion = f32[1,2,48,128,128]{4,3,2,1,0:T(8,128)} fusion(f32[1,48,128,128]{3,2,1,0:T(8,128)S(1)} %convolution_bitcast_fusion, f32[1,48,128,128]{3,2,1,0:T(8,128)S(1)} %convolution_bitcast_fusion.1), kind=kLoop, calls=%fused_computation | loop fusion | flops 1572864 | bytes 12582912 | tf_op jit(solution)/shard_map/while/body/jit(dynamic_update_index_in_dim)/broadcast_in_dim | solution.py:60
  23.2 0.0 copy-start.1
  23.2 0.0 all-reduce.3.cloned.1.call-update
  23.9 0.0 copy-done.1
  23.9 0.6 dynamic-slice
  25.1 119.0 %all-reduce.3.cloned.1.call-done = f32[1,2,48,128,128]{4,3,2,1,0:T(8,128)} async-done(((f32[1,2,48,128,128]{4,3,2,1,0:T(8,128)}), f32[1,2,48,128,128]{4,3,2,1,0:T(8,128)}) %all-reduce.3.cloned.1.call-update) | async-done | bytes 6291472
  144.1 2.7 %dynamic-slice_multiply_fusion = f32[1,2,12,128,128]{4,3,2,1,0:T(8,128)} fusion(f32[1,2,48,128,128]{4,3,2,1,0:T(8,128)} %all-reduce.3.cloned.1.call-done, u32[]{:T(128)S(6)} %multiply.11, f32[]{:T(128)} %bitcast.12), kind=kLoop, calls=%fused_computation.3 | loop fusion | flops 393216 | bytes 3145736 | tf_op jit(solution)/shard_map/mul | solution.py:75
  (7 shorter events, 0.1 us)
Async XLA Ops:
  6.5 1.0 copy-start
  6.5 137.6 %all-reduce.3.cloned.1.call-start = ((), (), s32[]{:S(2)}) async-start(), calls=%async_computation | async-start | bytes 12582912
  7.9 8.7 %collective-permute-start = (bf16[1,2,48,256]{3,2,1,0:T(8,128)(2,1)S(1)}, bf16[1,2,48,256]{3,2,1,0:T(8,128)(2,1)S(1)}, u32[]{:S(2)}, u32[]{:S(2)}) collective-permute-start(bf16[1,2,48,256]{3,2,1,0:T(8,128)(2,1)S(1)} %fusion.11), channel_id=1, source_target_pairs={{0,4},{4,8},{8,12},{12,16},{16,20},{20,24},{24,28},{1,5},{5,9},{9,... | collective-permute-start | bytes 147464 | tf_op jit(solution)/shard_map/ppermute | solution.py:21
  12.8 6.0 %collective-permute-start.1 = (bf16[1,2,48,256]{3,2,1,0:T(8,128)(2,1)S(1)}, bf16[1,2,48,256]{3,2,1,0:T(8,128)(2,1)S(1)}, u32[]{:S(2)}, u32[]{:S(2)}) collective-permute-start(bf16[1,2,48,256]{3,2,1,0:T(8,128)(2,1)S(1)} %fusion.11), channel_id=1, source_target_pairs={{4,0},{8,4},{12,8},{16,12},{20,16},{24,20},{28,24},{5,1},{9,5},{13... | collective-permute-start | bytes 147464 | tf_op jit(solution)/shard_map/ppermute | solution.py:23
  23.2 0.7 copy-start.1
Sparse Core Ops, SparseCore 0:
  23.3 120.7 all-reduce.2
where the time goes:
time: 154 us
  waiting for transfers between devices  121 us (79%)
  between operations  16 us (10%)
  other arithmetic  6.7 us (4%)
  starting transfers between devices  6.14 us (4%)
  local copies, waits for them, and re-layouts  2.09 us (1%)
  matrix products  1.57 us (1%)
    unnamed x2, waiting for transfers between devices  119 us
    ppermute x1, starting transfers between devices, with_halo(): lax.ppermute(tail, axis, [(i, (i + 1) % count) for i in range(ends)])  4.84 us
  transfers between devices with their start and end apart: 3, of which 2 were waited for; matrix products, arithmetic and copies ran while one was open for 1% of the time, Pallas kernels for 0%

commit v1 on v0

v1 whole, which is shorter than its diff:
```python
import functools
import math

import jax
import jax.numpy as jnp
import ml_dtypes
import numpy as np
from jax import lax
from jax.experimental import pallas as pl
from jax.experimental.pallas import tpu as pltpu
from jax.sharding import PartitionSpec as P

CH = 128
BINS = 48
FIRST_BIN = 8
MESH = pl.DeviceIdType.MESH


def spectra_rows(samples, wins):
    bins_here = BINS // wins
    depth = -(-2 * bins_here // 8) * 8
    times = np.arange(samples, dtype=np.int32)[None, :]
    freqs = FIRST_BIN + np.arange(BINS, dtype=np.int32)[:, None]
    phase = (times * freqs % samples).astype(np.float32) * np.float32(2.0 * math.pi / samples)
    both = np.stack([np.cos(phase), -np.sin(phase)], 1).astype(ml_dtypes.bfloat16)
    rows = np.zeros((wins, depth, samples), ml_dtypes.bfloat16)
    rows[:, : 2 * bins_here] = both.reshape(wins, 2 * bins_here, samples)
    return rows.reshape(wins * depth, samples)


def exchange(blks, wins, depth, x_ref, table_ref, white, held, send_sem, recv_sem):
    blk = lax.axis_index("blk")
    win = lax.axis_index("win")
    sides = ((-1, blk > 0), (1, blk < blks - 1))

    barrier = pltpu.get_barrier_semaphore()

    def greet(step, first):
        for j in range(first, wins):
            pl.semaphore_signal(
                barrier,
                inc=1,
                device_id=(blk + step, lax.rem(win + j, wins)),
                device_id_type=MESH,
            )

    for step, there in sides:
        pl.when(there)(functools.partial(greet, step, 0))
    greet(0, 1)

    spec = lax.dot_general(
        table_ref[...], x_ref[...], (((1,), (1,)), ((), ())), preferred_element_type=jnp.float32
    )
    energy = jnp.sum(spec * spec, axis=0, keepdims=True) * (1.0 / (2 * BINS))
    whitened = spec * lax.rsqrt(energy + 1e-06)
    for v in range(wins):
        part = whitened[v * depth : (v + 1) * depth]
        white[v] = jnp.concatenate(
            [part[:, b * CH : (b + 1) * CH] for b in range(part.shape[1] // CH)], 0
        ).astype(jnp.bfloat16)

    partners = (wins - 1) + wins * ((blk > 0).astype(jnp.int32) + (blk < blks - 1).astype(jnp.int32))
    pl.semaphore_wait(barrier, partners)

    def copy(step, j):
        v = lax.rem(win + j, wins)
        return pltpu.make_async_remote_copy(
            src_ref=white.at[v],
            dst_ref=held.at[1 - step, win],
            send_sem=send_sem.at[1 + step, j],
            recv_sem=recv_sem.at[1 - step, win],
            device_id=(blk + step, v),
            device_id_type=MESH,
        )

    def arrival(step, j):
        v = lax.rem(win + j, wins)
        return pltpu.make_async_remote_copy(
            src_ref=white.at[v],
            dst_ref=held.at[1 + step, v],
            send_sem=send_sem.at[1 + step, j],
            recv_sem=recv_sem.at[1 + step, v],
            device_id=(blk + step, v),
            device_id_type=MESH,
        )

    def each(make, act):
        def side(step, first):
            for j in range(first, wins):
                getattr(make(step, j), act)()

        for step, there in sides:
            pl.when(there)(functools.partial(side, step, 0))
        side(0, 1)

    each(copy, "start")
    held[1, win] = white[win]
    each(arrival, "wait_recv")
    return lambda: each(copy, "wait_send")


def cross(blks, wins, depth, pairs_ref, held, out_ref):
    blk = lax.axis_index("blk")
    blocks_here = held.shape[2] // depth
    bins_here = BINS // wins
    first, second = pairs_ref[0, 0], pairs_ref[0, 1]
    live = first >= 0

    def block(index):
        place = jnp.where(live, index - (blk - 1) * blocks_here, blocks_here)
        place = jnp.clip(place, 0, 3 * blocks_here - 1)
        rows = held[place // blocks_here].astype(jnp.float32)
        which = place % blocks_here
        chosen = rows[:, :depth]
        for b in range(1, blocks_here):
            chosen = jnp.where(which == b, rows[:, b * depth : (b + 1) * depth], chosen)
        return chosen.reshape(wins * depth, CH)

    a = block(first)
    b = block(second)
    count = wins * depth
    odd = lax.broadcasted_iota(jnp.int32, (count, CH), 0) % 2
    turned = jnp.where(odd == 1, pltpu.roll(b, 1, 0), -pltpu.roll(b, count - 1, 0))
    right = jnp.concatenate([b, turned], 1).astype(jnp.bfloat16)
    left = a.T
    bin_of = (lax.broadcasted_iota(jnp.int32, (CH, count), 1) % depth) // 2
    lefts = jnp.concatenate(
        [jnp.where(bin_of == k, left, 0.0).astype(jnp.bfloat16) for k in range(bins_here)], 0
    )
    both = jnp.dot(lefts, right, preferred_element_type=jnp.float32)
    both = both * jnp.where(live, 1.0 / math.sqrt(wins), 0.0).astype(jnp.float32)
    for k in range(bins_here):
        rows = both[k * CH : (k + 1) * CH]
        out_ref[0, k] = rows[:, :CH]
        out_ref[1, k] = rows[:, CH:]


def kernel(blks, wins, depth, pairs_ref, x_ref, table_ref, out_ref, white, held, send_sem, recv_sem):
    finish = exchange(blks, wins, depth, x_ref, table_ref, white, held, send_sem, recv_sem)
    cross(blks, wins, depth, pairs_ref, held, out_ref)
    finish()


def solution(mesh):
    blks, wins = mesh.shape["blk"], mesh.shape["win"]

    def shards(traces, pairs):
        rows, windows, samples = traces.shape
        assert windows == 1 and pairs.shape[0] == 1
        table = spectra_rows(samples, wins)
        depth = table.shape[0] // wins
        packed = rows // CH * depth
        bins_here = BINS // wins
        out = pl.pallas_call(
            functools.partial(kernel, blks, wins, depth),
            out_shape=jax.ShapeDtypeStruct((2, bins_here, CH, CH), jnp.float32),
            in_specs=[
                pl.BlockSpec(memory_space=pltpu.SMEM),
                pl.BlockSpec(memory_space=pltpu.VMEM),
                pl.BlockSpec(memory_space=pltpu.VMEM),
            ],
            out_specs=pl.BlockSpec(memory_space=pltpu.VMEM),
            scratch_shapes=[
                pltpu.VMEM((wins, packed, CH), jnp.bfloat16),
                pltpu.VMEM((3, wins, packed, CH), jnp.bfloat16),
                pltpu.SemaphoreType.DMA((3, wins)),
                pltpu.SemaphoreType.DMA((3, wins)),
            ],
            compiler_params=pltpu.CompilerParams(
                collective_id=0, has_side_effects=True, vmem_limit_bytes=24 << 20
            ),
        )(pairs, traces.reshape(rows, samples), jnp.asarray(table))
        return out[None]

    return jax.shard_map(
        shards,
        mesh=mesh,
        in_specs=(P("blk", "win", None), P("blk", None)),
        out_specs=P("blk", None, "win", None, None),
        check_vma=False,
    )
```

time: 154 us -> 12.7 us (0.08)
  waiting for transfers between devices: 121 us -> 0 us
  between operations: 16 us -> 0.01 us
  Pallas kernels: 0 us -> 8.74 us
  other arithmetic: 6.7 us -> 0 us
  starting transfers between devices: 6.14 us -> 0 us
  local copies, waits for them, and re-layouts: 2.09 us -> 3.77 us
  matrix products: 1.57 us -> 0 us
    unnamed x2 -> x0, waiting for transfers between devices: 119 us -> none
    pallas_call x0 -> x1, Pallas kernels: none -> 8.74 us  [shards(): pl.pallas_call(functools.partial(kernel, blks, wins, depth), out_shape=ja...]
    ppermute x2 -> x0, starting transfers between devices: 6.14 us -> none  [the longest x1 4.84 us: with_halo(): lax.ppermute(tail, axis, [(i, (i + 1) % count) for i in range(ends)])]
    broadcast_in_dim x1 -> x0, other arithmetic: 3.06 us -> none  [correlate(): return lax.map(one_pair, pairs)]
    unnamed x5 -> x7, local copies, waits for them, and re-layouts: 0.76 us -> 3.77 us
    mul x1 -> x0, other arithmetic: 2.73 us -> none  [shards(): summed * (1.0 / math.sqrt(windows_all)) * live[:, None, None, None, None]]
    ppermute x2 -> x0, waiting for transfers between devices: 2.14 us -> none  [the longest x1 2.14 us: with_halo(): lax.ppermute(head, axis, [((i + 1) % count, i) for i in range(ends)])]
    dot_general x3 -> x0, matrix products: 1.57 us -> none  [the longest x1 0.63 us: cross_pair(): jnp.einsum('kfi,kfj->fij', turned_left, turned_right, preferred_element_t...]
  transfers between devices with their start and end apart: 3 -> 0, of which waited for: 2 -> 0; matrix products, arithmetic and copies ran while one was open for 1% -> 0% of each run, Pallas kernels for 0% -> 0%
where the time goes in v1:
time: 12.7 us; the launch traced here: 12.5 us
  Pallas kernels  8.74 us (69%)
  local copies, waits for them, and re-layouts  3.77 us (30%)
    pallas_call x1, Pallas kernels, shards(): pl.pallas_call(functools.partial(kernel, blks, wins, depth), out_shape=ja...  8.74 us
    unnamed x7, local copies, waits for them, and re-layouts  3.77 us

profile of v1, /device:TPU:0, one launch (start us, length us, event | category | flops | bytes accessed | tf_op | source)
XLA Modules:
  0.0 12.5 jit_solution(7466306753203559033)
XLA Ops:
  0.0 0.0 copy-start
  0.0 1.0 %copy-done = bf16[256,1,1024]{2,0,1:T(8,128)(2,1)S(1)} copy-done((bf16[256,1,1024]{2,0,1:T(8,128)(2,1)S(1)}, bf16[256,1,1024]{2,0,1:T(8,128)(2,1)}, u32[]{:S(2)}) %copy-start) | copy-done | bytes 524312
  1.0 0.0 copy-start.1
  1.0 0.9 %copy-done.1 = bf16[96,1024]{1,0:T(8,128)(2,1)S(1)} copy-done((bf16[96,1024]{1,0:T(8,128)(2,1)S(1)}, bf16[96,1024]{1,0:T(8,128)(2,1)}, u32[]{:S(2)}) %copy-start.1) | copy-done | bytes 196632
  2.0 0.0 copy-start.2
  2.0 0.7 %copy-done.2 = s32[1,2]{1,0:T(1,128)S(1)} copy-done((s32[1,2]{1,0:T(1,128)S(1)}, s32[1,2]{1,0:T(1,128)}, u32[]{:S(2)}) %copy-start.2) | copy-done | bytes 32
  2.6 8.7 %shard_map.37 = f32[2,12,128,128]{3,2,1,0:T(8,128)S(1)} custom-call(s32[1,2]{1,0:T(1,128)S(1)} %copy-done.2, bf16[256,1024]{1,0:T(8,128)(2,1)S(1)} %bitcast.3, bf16[96,1024]{1,0:T(8,128)(2,1)S(1)} %copy-done.1), custom_call_target="tpu_custom_call" | custom-call | tf_op jit(solution)/shard_map/pallas_call | solution.py:154
  11.4 1.1 %copy.5 = f32[1,2,12,128,128]{4,3,2,1,0:T(8,128)} copy(f32[1,2,12,128,128]{4,3,2,1,0:T(8,128)S(1)} %bitcast.2) | data formatting | bytes 3145728
Async XLA Ops:
  0.0 1.0 %copy-start = (bf16[256,1,1024]{2,0,1:T(8,128)(2,1)S(1)}, bf16[256,1,1024]{2,0,1:T(8,128)(2,1)}, u32[]{:S(2)}) copy-start(bf16[256,1,1024]{2,0,1:T(8,128)(2,1)} %param.3) | copy-start | bytes 1572868
  1.0 0.9 %copy-start.1 = (bf16[96,1024]{1,0:T(8,128)(2,1)S(1)}, bf16[96,1024]{1,0:T(8,128)(2,1)}, u32[]{:S(2)}) copy-start(bf16[96,1024]{1,0:T(8,128)(2,1)} %constant.2.clone.table_ref) | copy-start | bytes 589828
  2.0 0.7 %copy-start.2 = (s32[1,2]{1,0:T(1,128)S(1)}, s32[1,2]{1,0:T(1,128)}, u32[]{:S(2)}) copy-start(s32[1,2]{1,0:T(1,128)} %pairs_ref.1) | copy-start | bytes 28

commit v2 on v1

--- a/solution.py
+++ b/solution.py
@@ -28,7 +28,7 @@
     return rows.reshape(wins * depth, samples)
 
 
-def exchange(blks, wins, depth, x_ref, table_ref, white, held, send_sem, recv_sem):
+def exchange(blks, wins, depth, x_ref, table_ref, white, held, send_sem, recv_sem, loaded):
     blk = lax.axis_index("blk")
     win = lax.axis_index("win")
     sides = ((-1, blk > 0), (1, blk < blks - 1))
@@ -48,6 +48,7 @@
         pl.when(there)(functools.partial(greet, step, 0))
     greet(0, 1)
 
+    loaded()
     spec = lax.dot_general(
         table_ref[...], x_ref[...], (((1,), (1,)), ((), ())), preferred_element_type=jnp.float32
     )
@@ -99,10 +100,9 @@
     return lambda: each(copy, "wait_send")
 
 
-def cross(blks, wins, depth, pairs_ref, held, out_ref):
+def operands(wins, depth, pairs_ref, held, left_ref, right_ref):
     blk = lax.axis_index("blk")
     blocks_here = held.shape[2] // depth
-    bins_here = BINS // wins
     first, second = pairs_ref[0, 0], pairs_ref[0, 1]
     live = first >= 0
 
@@ -116,29 +116,50 @@
             chosen = jnp.where(which == b, rows[:, b * depth : (b + 1) * depth], chosen)
         return chosen.reshape(wins * depth, CH)
 
-    a = block(first)
-    b = block(second)
     count = wins * depth
+    left_ref[...] = block(first).T.astype(jnp.bfloat16)
+    b = block(second) * jnp.where(live, 1.0 / math.sqrt(wins), 0.0).astype(jnp.float32)
     odd = lax.broadcasted_iota(jnp.int32, (count, CH), 0) % 2
     turned = jnp.where(odd == 1, pltpu.roll(b, 1, 0), -pltpu.roll(b, count - 1, 0))
-    right = jnp.concatenate([b, turned], 1).astype(jnp.bfloat16)
-    left = a.T
-    bin_of = (lax.broadcasted_iota(jnp.int32, (CH, count), 1) % depth) // 2
-    lefts = jnp.concatenate(
-        [jnp.where(bin_of == k, left, 0.0).astype(jnp.bfloat16) for k in range(bins_here)], 0
-    )
-    both = jnp.dot(lefts, right, preferred_element_type=jnp.float32)
-    both = both * jnp.where(live, 1.0 / math.sqrt(wins), 0.0).astype(jnp.float32)
+    right_ref[...] = jnp.concatenate([b, turned], 1).astype(jnp.bfloat16)
+
+
+def spectra_kernel(
+    blks, wins, depth, pairs_ref, x_ref, table_ref, left_ref, right_ref,
+    x, table, pairs, white, held, send_sem, recv_sem, load_sem,
+):
+    loads = [
+        pltpu.make_async_copy(src, dst, load_sem.at[i])
+        for i, (src, dst) in enumerate(((x_ref, x), (table_ref, table), (pairs_ref, pairs)))
+    ]
+    for load in loads:
+        load.start()
+
+    def loaded():
+        for load in loads:
+            load.wait()
+
+    finish = exchange(blks, wins, depth, x, table, white, held, send_sem, recv_sem, loaded)
+    operands(wins, depth, pairs, held, left_ref, right_ref)
+    finish()
+
+
+def cross_kernel(depth, left_ref, right_ref, out_ref, result, sem):
+    bins_here = result.shape[1]
+    left, right = left_ref[...], right_ref[...]
+    bin_of = (lax.broadcasted_iota(jnp.int32, left.shape, 1) % depth) // 2
+    writes = []
     for k in range(bins_here):
-        rows = both[k * CH : (k + 1) * CH]
-        out_ref[0, k] = rows[:, :CH]
-        out_ref[1, k] = rows[:, CH:]
-
-
-def kernel(blks, wins, depth, pairs_ref, x_ref, table_ref, out_ref, white, held, send_sem, recv_sem):
-    finish = exchange(blks, wins, depth, x_ref, table_ref, white, held, send_sem, recv_sem)
-    cross(blks, wins, depth, pairs_ref, held, out_ref)
-    finish()
+        both = jnp.dot(
+            jnp.where(bin_of == k, left, jnp.zeros_like(left)), right, preferred_element_type=jnp.float32
+        )
+        for c in range(2):
+            result[c, k] = both[:, c * CH : (c + 1) * CH]
+            write = pltpu.make_async_copy(result.at[c, k], out_ref.at[c, k], sem.at[c, k])
+            write.start()
+            writes.append(write)
+    for write in writes:
+        write.wait()
 
 
 def solution(mesh):
@@ -148,28 +169,44 @@
         rows, windows, samples = traces.shape
         assert windows == 1 and pairs.shape[0] == 1
         table = spectra_rows(samples, wins)
-        depth = table.shape[0] // wins
+        count = table.shape[0]
+        depth = count // wins
         packed = rows // CH * depth
         bins_here = BINS // wins
-        out = pl.pallas_call(
-            functools.partial(kernel, blks, wins, depth),
-            out_shape=jax.ShapeDtypeStruct((2, bins_here, CH, CH), jnp.float32),
-            in_specs=[
-                pl.BlockSpec(memory_space=pltpu.SMEM),
-                pl.BlockSpec(memory_space=pltpu.VMEM),
-                pl.BlockSpec(memory_space=pltpu.VMEM),
+        inputs = pairs, traces.reshape(rows, samples), jnp.asarray(table)
+        left, right = pl.pallas_call(
+            functools.partial(spectra_kernel, blks, wins, depth),
+            out_shape=[
+                pltpu.VMEM((CH, count), jnp.bfloat16),
+                pltpu.VMEM((count, 2 * CH), jnp.bfloat16),
             ],
-            out_specs=pl.BlockSpec(memory_space=pltpu.VMEM),
+            in_specs=[pl.BlockSpec(memory_space=pltpu.HBM)] * 3,
+            out_specs=[pl.BlockSpec(memory_space=pltpu.VMEM)] * 2,
             scratch_shapes=[
+                pltpu.VMEM((rows, samples), jnp.bfloat16),
+                pltpu.VMEM((count, samples), jnp.bfloat16),
+                pltpu.SMEM((1, 2), jnp.int32),
                 pltpu.VMEM((wins, packed, CH), jnp.bfloat16),
                 pltpu.VMEM((3, wins, packed, CH), jnp.bfloat16),
                 pltpu.SemaphoreType.DMA((3, wins)),
                 pltpu.SemaphoreType.DMA((3, wins)),
+                pltpu.SemaphoreType.DMA((3,)),
             ],
             compiler_params=pltpu.CompilerParams(
                 collective_id=0, has_side_effects=True, vmem_limit_bytes=24 << 20
             ),
-        )(pairs, traces.reshape(rows, samples), jnp.asarray(table))
+        )(*(pltpu.with_memory_space_constraint(a, pltpu.HBM) for a in inputs))
+        out = pl.pallas_call(
+            functools.partial(cross_kernel, depth),
+            out_shape=jax.ShapeDtypeStruct((2, bins_here, CH, CH), jnp.float32),
+            in_specs=[pl.BlockSpec(memory_space=pltpu.VMEM)] * 2,
+            out_specs=pl.BlockSpec(memory_space=pltpu.HBM),
+            scratch_shapes=[
+                pltpu.VMEM((2, bins_here, CH, CH), jnp.float32),
+                pltpu.SemaphoreType.DMA((2, bins_here)),
+            ],
+            compiler_params=pltpu.CompilerParams(vmem_limit_bytes=24 << 20),
+        )(left, right)
         return out[None]
 
     return jax.shard_map(

time: 12.7 us -> 9.4 us (0.74)
  local copies, waits for them, and re-layouts: 3.77 us -> 0 us
  Pallas kernels: 8.74 us -> 9.25 us
    unnamed x7 -> x0, local copies, waits for them, and re-layouts: 3.77 us -> none
    pallas_call x1 -> x2, Pallas kernels: 8.74 us -> 9.25 us  [the longest x1 7.74 us: shards(): pl.pallas_call(functools.partial(spectra_kernel, blks, wins, depth), out_...]
where the time goes in v2:
time: 9.4 us; the launch traced here: 9.26 us
  Pallas kernels  9.25 us (98%)
    pallas_call x1, Pallas kernels, shards(): pl.pallas_call(functools.partial(spectra_kernel, blks, wins, depth), out_...  7.74 us
    pallas_call x1, Pallas kernels, shards(): pl.pallas_call(functools.partial(cross_kernel, depth), out_shape=jax.Shap...  1.51 us

profile of v2, /device:TPU:0, one launch (start us, length us, event | category | flops | bytes accessed | tf_op | source)
XLA Modules:
  0.0 9.3 jit_solution(298545535749940386)
XLA Ops:
  0.0 7.7 %shard_map.37 = (bf16[128,96]{1,0:T(8,128)(2,1)S(1)}, bf16[96,256]{1,0:T(8,128)(2,1)S(1)}) custom-call(s32[1,2]{1,0:T(1,128)} %pairs_ref.1, bf16[256,1024]{1,0:T(8,128)(2,1)} %bitcast.2, bf16[96,1024]{1,0:T(8,128)(2,1)} %constant.2.clone.table_ref), custom_call_target="tpu_custom_call" | custom-call | tf_op jit(solution)/shard_map/pallas_call | solution.py:177
  7.8 1.5 %shard_map.38 = f32[2,12,128,128]{3,2,1,0:T(8,128)} custom-call(bf16[128,96]{1,0:T(8,128)(2,1)S(1)} %get-tuple-element.7.left_ref, bf16[96,256]{1,0:T(8,128)(2,1)S(1)} %get-tuple-element.8.right_ref), custom_call_target="tpu_custom_call" | custom-call | tf_op jit(solution)/shard_map/pallas_call | solution.py:199

commit v3 on v2

--- a/solution.py
+++ b/solution.py
@@ -63,8 +63,14 @@
     partners = (wins - 1) + wins * ((blk > 0).astype(jnp.int32) + (blk < blks - 1).astype(jnp.int32))
     pl.semaphore_wait(barrier, partners)
 
+    def target(step, j):
+        if step == 0 or wins % 2:
+            return lax.rem(win + j, wins)
+        half = wins // 2
+        return 2 * lax.rem(win // 2 + 1 + j % half, half) + j // half
+
     def copy(step, j):
-        v = lax.rem(win + j, wins)
+        v = target(step, j)
         return pltpu.make_async_remote_copy(
             src_ref=white.at[v],
             dst_ref=held.at[1 - step, win],
@@ -75,7 +81,7 @@
         )
 
     def arrival(step, j):
-        v = lax.rem(win + j, wins)
+        v = target(step, j)
         return pltpu.make_async_remote_copy(
             src_ref=white.at[v],
             dst_ref=held.at[1 + step, v],

time: 9.4 us -> 9.28 us (0.987)
  Pallas kernels: 9.25 us -> 9.12 us
    pallas_call x1, Pallas kernels: 7.74 us -> 7.61 us  [shards(): pl.pallas_call(functools.partial(spectra_kernel, blks, wins, depth), out_...]
where the time goes in v3:
time: 9.28 us; the launch traced here: 9.13 us
  Pallas kernels  9.12 us (98%)
    pallas_call x1, Pallas kernels, shards(): pl.pallas_call(functools.partial(spectra_kernel, blks, wins, depth), out_...  7.61 us
    pallas_call x1, Pallas kernels, shards(): pl.pallas_call(functools.partial(cross_kernel, depth), out_shape=jax.Shap...  1.51 us

profile of v3, /device:TPU:0, one launch (start us, length us, event | category | flops | bytes accessed | tf_op | source)
XLA Modules:
  0.0 9.1 jit_solution(11049113373587434909)
XLA Ops:
  0.0 7.6 %shard_map.37 = (bf16[128,96]{1,0:T(8,128)(2,1)S(1)}, bf16[96,256]{1,0:T(8,128)(2,1)S(1)}) custom-call(s32[1,2]{1,0:T(1,128)} %pairs_ref.1, bf16[256,1024]{1,0:T(8,128)(2,1)} %bitcast.2, bf16[96,1024]{1,0:T(8,128)(2,1)} %constant.2.clone.table_ref), custom_call_target="tpu_custom_call" | custom-call | tf_op jit(solution)/shard_map/pallas_call | solution.py:183
  7.6 1.5 %shard_map.38 = f32[2,12,128,128]{3,2,1,0:T(8,128)} custom-call(bf16[128,96]{1,0:T(8,128)(2,1)S(1)} %get-tuple-element.7.left_ref, bf16[96,256]{1,0:T(8,128)(2,1)S(1)} %get-tuple-element.8.right_ref), custom_call_target="tpu_custom_call" | custom-call | tf_op jit(solution)/shard_map/pallas_call | solution.py:205

commit v4 on v2

--- a/solution.py
+++ b/solution.py
@@ -35,12 +35,18 @@
 
     barrier = pltpu.get_barrier_semaphore()
 
+    def target(step, j):
+        if step == 0 or wins % 2:
+            return lax.rem(win + j, wins)
+        half = wins // 2
+        return 2 * lax.rem(win // 2 + 1 + j % half, half) + j // half
+
     def greet(step, first):
         for j in range(first, wins):
             pl.semaphore_signal(
                 barrier,
                 inc=1,
-                device_id=(blk + step, lax.rem(win + j, wins)),
+                device_id=(blk + step, target(step, j)),
                 device_id_type=MESH,
             )
 
@@ -64,7 +70,7 @@
     pl.semaphore_wait(barrier, partners)
 
     def copy(step, j):
-        v = lax.rem(win + j, wins)
+        v = target(step, j)
         return pltpu.make_async_remote_copy(
             src_ref=white.at[v],
             dst_ref=held.at[1 - step, win],
@@ -75,7 +81,7 @@
         )
 
     def arrival(step, j):
-        v = lax.rem(win + j, wins)
+        v = target(step, j)
         return pltpu.make_async_remote_copy(
             src_ref=white.at[v],
             dst_ref=held.at[1 + step, v],
@@ -86,13 +92,14 @@
         )
 
     def each(make, act):
-        def side(step, first):
-            for j in range(first, wins):
+        def side(step, js):
+            for j in js:
                 getattr(make(step, j), act)()
 
-        for step, there in sides:
-            pl.when(there)(functools.partial(side, step, 0))
-        side(0, 1)
+        for js in (range(wins // 2), range(wins // 2, wins)):
+            for step, there in sides:
+                pl.when(there)(functools.partial(side, step, js))
+        side(0, range(1, wins))
 
     each(copy, "start")
     held[1, win] = white[win]

time: 9.4 us -> 9.27 us (0.986)
  Pallas kernels: 9.25 us -> 9.12 us
    pallas_call x1, Pallas kernels: 7.74 us -> 7.61 us  [shards(): pl.pallas_call(functools.partial(spectra_kernel, blks, wins, depth), out_...]
where the time goes in v4:
time: 9.27 us; the launch traced here: 9.13 us
  Pallas kernels  9.12 us (98%)
    pallas_call x1, Pallas kernels, shards(): pl.pallas_call(functools.partial(spectra_kernel, blks, wins, depth), out_...  7.61 us
    pallas_call x1, Pallas kernels, shards(): pl.pallas_call(functools.partial(cross_kernel, depth), out_shape=jax.Shap...  1.51 us

profile of v4, /device:TPU:0, one launch (start us, length us, event | category | flops | bytes accessed | tf_op | source)
XLA Modules:
  0.0 9.1 jit_solution(16126696477806729415)
XLA Ops:
  0.0 7.6 %shard_map.37 = (bf16[128,96]{1,0:T(8,128)(2,1)S(1)}, bf16[96,256]{1,0:T(8,128)(2,1)S(1)}) custom-call(s32[1,2]{1,0:T(1,128)} %pairs_ref.1, bf16[256,1024]{1,0:T(8,128)(2,1)} %bitcast.2, bf16[96,1024]{1,0:T(8,128)(2,1)} %constant.2.clone.table_ref), custom_call_target="tpu_custom_call" | custom-call | tf_op jit(solution)/shard_map/pallas_call | solution.py:184
  7.6 1.5 %shard_map.38 = f32[2,12,128,128]{3,2,1,0:T(8,128)} custom-call(bf16[128,96]{1,0:T(8,128)(2,1)S(1)} %get-tuple-element.7.left_ref, bf16[96,256]{1,0:T(8,128)(2,1)S(1)} %get-tuple-element.8.right_ref), custom_call_target="tpu_custom_call" | custom-call | tf_op jit(solution)/shard_map/pallas_call | solution.py:206
